TPU v7x, 256 devices: a whole 4x4x8 slice. The times are simulated.
256 devices in a mesh: cols: 64 (over x_hi, z, y), rows: 4 (over x_lo, core).
Axes of the slice: x: 4 (x_hi: 2, x_lo: 2; x = x_hi * 2 + x_lo), y: 4, z: 8, core: 2. Of those that a mesh axis runs over, the one named last changes fastest.
Arguments:
- image: bfloat16 [64, 1024, 512], P('rows', 'cols'), may hold values from -6 to 6
- w_qkv: bfloat16 [512, 1536], replicated, may hold values from -0.25 to 0.25
- b_qkv: float32 [1536], replicated, may hold values from -3 to 3
- logit_scale: float32 [16], replicated, may hold values from 0.7 to 3
- bias_table: float32 [16, 961], replicated, may hold values from -5 to 5
- w_proj: bfloat16 [512, 512], replicated, may hold values from -0.25 to 0.25
- b_proj: float32 [512], replicated, may hold values from -3 to 3
- gain_attn: float32 [512], replicated, may hold values from 0.25 to 1.75
- shift_attn: float32 [512], replicated, may hold values from -3 to 3
- w_merge: bfloat16 [2048, 1024], replicated, may hold values from -0.125 to 0.125
- gain_merge: float32 [1024], replicated, may hold values from 0.25 to 1.75
- shift_merge: float32 [1024], replicated, may hold values from -3 to 3
- grad_out: bfloat16 [32, 512, 1024], P('rows', 'cols'), may hold values from -6 to 6
Outputs:
- merged: bfloat16 [32, 512, 1024], P('rows', 'cols')
- grad_image: bfloat16 [64, 1024, 512], P('rows', 'cols')
- grad_qkv: float32 [786432], P(('cols', 'rows'))
- grad_proj: float32 [262144], P(('cols', 'rows'))
- grad_merge: float32 [2097152], P(('cols', 'rows'))
All inputs are finite; a program needn't handle non-finite values.
Results may differ from a plain program's by a relative error of at most 0.013.
Values may be sent and summed in bfloat16 or wider, within the bound.
A program may use at most 128 MiB of HBM per device.

v0:
```python
import math

import jax
import jax.numpy as jnp
from jax import lax
from jax.sharding import PartitionSpec as P

WIN = 16


EPS_NORM = 1e-05
EPS_COS = 1e-06
HIGH = lax.Precision.HIGHEST


def from_behind(value, axis, steps):
    count = lax.axis_size(axis)
    pairs = [(source, (source + steps) % count) for source in range(count)]
    return lax.ppermute(value, axis, pairs)


def low_einsum(form, left, right):
    return jnp.einsum(form, left, right, preferred_element_type=jnp.float32)


def contract_rows(left, right):
    return lax.dot_general(
        left, right, (((0,), (0,)), ((), ())), preferred_element_type=jnp.float32
    )


def contract_cols(left, right):
    return lax.dot_general(
        left, right, (((1,), (1,)), ((), ())), preferred_element_type=jnp.float32
    )


def layer_forward(values, gain_vec, offset):
    average = jnp.mean(values, axis=-1, keepdims=True)
    centered = values - average
    inverse = lax.rsqrt(jnp.mean(centered * centered, axis=-1, keepdims=True) + EPS_NORM)
    normed = centered * inverse
    return (normed * gain_vec + offset, normed, inverse)


def layer_backward(normed, inverse, gain_vec, upstream):
    scaled = upstream * gain_vec
    mean_term = jnp.mean(scaled, axis=-1, keepdims=True)
    proj_term = jnp.mean(scaled * normed, axis=-1, keepdims=True)
    return inverse * (scaled - mean_term - normed * proj_term)


def partition(grid, window):
    rows_n, cols_n, depth = grid.shape
    split = grid.reshape(rows_n // window, window, cols_n // window, window, depth)
    return split.transpose(0, 2, 1, 3, 4).reshape(-1, window * window, depth)


def unpartition(windows, rows_n, cols_n, window):
    depth = windows.shape[-1]
    split = windows.reshape(rows_n // window, cols_n // window, window, window, depth)
    return split.transpose(0, 2, 1, 3, 4).reshape(rows_n, cols_n, depth)


def region_of(coords, total, window):
    return (coords >= total - window).astype(jnp.int32) + (coords >= total - window // 2).astype(
        jnp.int32
    )


def bias_from_table(table, window):
    head_count = table.shape[0]
    span_len = 2 * window - 1
    grid_table = table.reshape(head_count, span_len, span_len)
    inside = jnp.arange(window, dtype=jnp.int32)
    offsets = inside[:, None] - inside[None, :] + window - 1
    onehot = (offsets[:, :, None] == jnp.arange(span_len, dtype=jnp.int32)[None, None, :]).astype(
        jnp.float32
    )
    by_rows = jnp.einsum("rta,hab->hrtb", onehot, grid_table, precision=HIGH)
    full = jnp.einsum("csb,hrtb->hrcts", onehot, by_rows, precision=HIGH)
    return 16.0 * jax.nn.sigmoid(full.reshape(head_count, window * window, window * window))


def make_allowed(region_windows):
    return (region_windows[:, :, None] == region_windows[:, None, :]).astype(jnp.float32)


def relocate(tile, strip, direction):
    if direction < 0:
        sent_cols = tile[:, :strip]
        kept_cols = tile[:, strip:]
    else:
        sent_cols = tile[:, -strip:]
        kept_cols = tile[:, :-strip]
    came_cols = from_behind(sent_cols, "cols", direction)
    if direction < 0:
        spread = jnp.concatenate([kept_cols, came_cols], axis=1)
        sent_rows = spread[:strip]
        kept_rows = spread[strip:]
    else:
        spread = jnp.concatenate([came_cols, kept_cols], axis=1)
        sent_rows = spread[-strip:]
        kept_rows = spread[:-strip]
    came_rows = from_behind(sent_rows, "rows", direction)
    if direction < 0:
        return jnp.concatenate([kept_rows, came_rows], axis=0)
    return jnp.concatenate([came_rows, kept_rows], axis=0)


def attend(
    windows, allowed, w_qkv, b_qkv, logit_scale, head_bias, w_proj, b_proj, gain_attn, shift_attn
):
    win_count, pixels, channels = windows.shape
    head_count = logit_scale.shape[0]
    head_dim = channels // head_count
    flat_rows = windows.reshape(win_count * pixels, channels)
    mixed = jnp.dot(flat_rows, w_qkv, preferred_element_type=jnp.float32) + b_qkv
    mixed = mixed.reshape(win_count, pixels, 3, head_count, head_dim)
    queries = mixed[:, :, 0]
    key_vecs = mixed[:, :, 1]
    value_low = mixed[:, :, 2].astype(jnp.bfloat16)
    query_inv = lax.rsqrt(jnp.sum(queries * queries, axis=-1, keepdims=True) + EPS_COS)
    key_inv = lax.rsqrt(jnp.sum(key_vecs * key_vecs, axis=-1, keepdims=True) + EPS_COS)
    query_unit = queries * query_inv
    key_unit = key_vecs * key_inv
    scale_vec = jnp.exp(logit_scale)[None, :, None, None]
    scores = (
        jnp.einsum("wphd,wqhd->whpq", query_unit, key_unit, precision=HIGH) * scale_vec
        + head_bias[None]
    )
    raised = jnp.exp(scores) * allowed[:, None]
    soft = raised / jnp.sum(raised, axis=-1, keepdims=True)
    soft_low = soft.astype(jnp.bfloat16)
    attended = low_einsum("whpq,wqhd->wphd", soft_low, value_low)
    attended_low = attended.astype(jnp.bfloat16).reshape(win_count * pixels, channels)
    projected = jnp.dot(attended_low, w_proj, preferred_element_type=jnp.float32) + b_proj
    branch, normed, inverse = layer_forward(projected, gain_attn, shift_attn)
    output = (flat_rows.astype(jnp.float32) + branch).astype(jnp.bfloat16)
    saved = (
        flat_rows,
        query_unit,
        key_unit,
        query_inv,
        key_inv,
        value_low,
        soft,
        soft_low,
        attended_low,
        normed,
        inverse,
    )
    return (output.reshape(win_count, pixels, channels), saved)


def attend_back(saved, upstream_low, w_qkv, logit_scale, w_proj, gain_attn):
    (
        flat_rows,
        query_unit,
        key_unit,
        query_inv,
        key_inv,
        value_low,
        soft,
        soft_low,
        attended_low,
        normed,
        inverse,
    ) = saved
    win_count, pixels, head_count, head_dim = query_unit.shape
    channels = head_count * head_dim
    upstream = upstream_low.astype(jnp.float32).reshape(win_count * pixels, channels)
    d_projected = layer_backward(normed, inverse, gain_attn, upstream).astype(jnp.bfloat16)
    grad_proj = contract_rows(attended_low, d_projected)
    d_attended = (
        contract_cols(d_projected, w_proj)
        .astype(jnp.bfloat16)
        .reshape(win_count, pixels, head_count, head_dim)
    )
    d_soft = low_einsum("wphd,wqhd->whpq", d_attended, value_low)
    d_value = low_einsum("whpq,wphd->wqhd", soft_low, d_attended)
    d_scores = soft * (d_soft - jnp.sum(soft * d_soft, axis=-1, keepdims=True))
    d_scaled = d_scores * jnp.exp(logit_scale)[None, :, None, None]
    d_qunit = jnp.einsum("whpq,wqhd->wphd", d_scaled, key_unit, precision=HIGH)
    d_kunit = jnp.einsum("whpq,wphd->wqhd", d_scaled, query_unit, precision=HIGH)
    d_query = query_inv * (
        d_qunit - query_unit * jnp.sum(query_unit * d_qunit, axis=-1, keepdims=True)
    )
    d_key = key_inv * (d_kunit - key_unit * jnp.sum(key_unit * d_kunit, axis=-1, keepdims=True))
    d_mixed = (
        jnp.stack([d_query, d_key, d_value], axis=2)
        .reshape(win_count * pixels, 3 * channels)
        .astype(jnp.bfloat16)
    )
    grad_qkv = contract_rows(flat_rows, d_mixed)
    d_rows = contract_cols(d_mixed, w_qkv)
    d_windows = (upstream + d_rows).astype(jnp.bfloat16)
    return (d_windows.reshape(win_count, pixels, channels), grad_qkv, grad_proj)


def merge_tokens(grid):
    rows_n, cols_n, channels = grid.shape
    parts = grid.reshape(rows_n // 2, 2, cols_n // 2, 2, channels)
    return jnp.concatenate(
        [parts[:, 0, :, 0], parts[:, 1, :, 0], parts[:, 0, :, 1], parts[:, 1, :, 1]], axis=-1
    )


def split_tokens(merged_grad):
    half_rows, half_cols, wide = merged_grad.shape
    channels = wide // 4
    quarter = merged_grad.reshape(half_rows, half_cols, 4, channels)
    upper = jnp.stack([quarter[:, :, 0], quarter[:, :, 2]], axis=2)
    lower = jnp.stack([quarter[:, :, 1], quarter[:, :, 3]], axis=2)
    return jnp.stack([upper, lower], axis=1).reshape(half_rows * 2, half_cols * 2, channels)


def merge_forward(grid, w_merge, gain_merge, shift_merge):
    gathered = merge_tokens(grid)
    half_rows, half_cols, wide = gathered.shape
    flat_in = gathered.reshape(half_rows * half_cols, wide)
    reduced = jnp.dot(flat_in, w_merge, preferred_element_type=jnp.float32)
    output, normed, inverse = layer_forward(reduced, gain_merge, shift_merge)
    return (
        output.astype(jnp.bfloat16).reshape(half_rows, half_cols, -1),
        (flat_in, normed, inverse),
    )


def merge_backward(saved, upstream_low, w_merge, gain_merge):
    flat_in, normed, inverse = saved
    half_rows, half_cols, out_width = upstream_low.shape
    upstream = upstream_low.astype(jnp.float32).reshape(half_rows * half_cols, out_width)
    d_reduced = layer_backward(normed, inverse, gain_merge, upstream).astype(jnp.bfloat16)
    grad_merge = contract_rows(flat_in, d_reduced)
    d_in = contract_cols(d_reduced, w_merge).astype(jnp.bfloat16)
    return (split_tokens(d_in.reshape(half_rows, half_cols, -1)), grad_merge)


def per_device(
    image,
    w_qkv,
    b_qkv,
    logit_scale,
    bias_table,
    w_proj,
    b_proj,
    gain_attn,
    shift_attn,
    w_merge,
    gain_merge,
    shift_merge,
    grad_out,
):
    rows_tile, cols_tile, channels = image.shape
    half = WIN // 2
    pixels = WIN * WIN
    row_devices = lax.axis_size("rows")
    col_devices = lax.axis_size("cols")
    shifted = relocate(image, half, -1)
    row_ids = lax.axis_index("rows") * rows_tile + jnp.arange(rows_tile, dtype=jnp.int32)
    col_ids = lax.axis_index("cols") * cols_tile + jnp.arange(cols_tile, dtype=jnp.int32)
    row_reg = region_of(row_ids, rows_tile * row_devices, WIN)
    col_reg = region_of(col_ids, cols_tile * col_devices, WIN)
    region = (row_reg[:, None] * 3 + col_reg[None, :])[:, :, None]
    reg_windows = partition(region, WIN)[:, :, 0]
    head_bias = bias_from_table(bias_table, WIN)
    win_all = partition(shifted, WIN)
    count = win_all.shape[0]
    group = math.gcd(count, 4)
    win_blocks = win_all.reshape(count // group, group, pixels, channels)
    reg_blocks = reg_windows.reshape(count // group, group, pixels)

    def forward_block(pieces):
        output, saved = attend(
            pieces[0],
            make_allowed(pieces[1]),
            w_qkv,
            b_qkv,
            logit_scale,
            head_bias,
            w_proj,
            b_proj,
            gain_attn,
            shift_attn,
        )
        return output

    out_blocks = lax.map(forward_block, (win_blocks, reg_blocks))
    shifted_out = unpartition(
        out_blocks.reshape(count, pixels, channels), rows_tile, cols_tile, WIN
    )
    result = relocate(shifted_out, half, 1)
    merged, merge_saved = merge_forward(result, w_merge, gain_merge, shift_merge)
    d_result, grad_merge = merge_backward(merge_saved, grad_out, w_merge, gain_merge)
    d_shifted = relocate(d_result, half, -1)
    factor = 1.0 / math.sqrt(rows_tile * cols_tile * row_devices * col_devices // 4)
    d_blocks = partition(d_shifted, WIN).reshape(count // group, group, pixels, channels)

    def backward_block(carry, pieces):
        output, saved = attend(
            pieces[0],
            make_allowed(pieces[1]),
            w_qkv,
            b_qkv,
            logit_scale,
            head_bias,
            w_proj,
            b_proj,
            gain_attn,
            shift_attn,
        )
        d_windows, grad_qkv, grad_proj = attend_back(
            saved, pieces[2], w_qkv, logit_scale, w_proj, gain_attn
        )
        return ((carry[0] + grad_qkv, carry[1] + grad_proj), d_windows)

    start = (
        jnp.zeros((channels, 3 * channels), jnp.float32),
        jnp.zeros((channels, channels), jnp.float32),
    )
    grads, d_win_blocks = lax.scan(backward_block, start, (win_blocks, reg_blocks, d_blocks))
    d_windows = d_win_blocks.reshape(count, pixels, channels)
    grad_image = relocate(unpartition(d_windows, rows_tile, cols_tile, WIN), half, 1)
    qkv_sum, proj_sum, merge_sum = (
        lax.psum_scatter(grads[0].reshape(-1), ("cols", "rows"), scatter_dimension=0, tiled=True),
        lax.psum_scatter(grads[1].reshape(-1), ("cols", "rows"), scatter_dimension=0, tiled=True),
        lax.psum_scatter(grad_merge.reshape(-1), ("cols", "rows"), scatter_dimension=0, tiled=True),
    )
    return (merged, grad_image, qkv_sum * factor, proj_sum * factor, merge_sum * factor)


def solution(mesh):
    placed = (
        P("rows", "cols", None),
        P(),
        P(),
        P(),
        P(),
        P(),
        P(),
        P(),
        P(),
        P(),
        P(),
        P(),
        P("rows", "cols", None),
    )
    return jax.shard_map(
        per_device,
        mesh=mesh,
        in_specs=placed,
        out_specs=(
            P("rows", "cols", None),
            P("rows", "cols", None),
            P(("cols", "rows")),
            P(("cols", "rows")),
            P(("cols", "rows")),
        ),
        check_vma=False,
    )
```

profile of v0, /device:TPU:1, one launch (start us, length us, event | category | flops | bytes accessed | tf_op | source)
XLA Modules:
  0.0 458.3 jit_solution(7396856924381863480)
XLA Ops:
  7.2 1.1 fusion.57
  8.3 11.4 %collective-permute-start = (bf16[16,8,512]{2,1,0:T(8,128)(2,1)S(1)}, bf16[16,8,512]{2,1,0:T(8,128)(2,1)S(1)}, u32[]{:S(2)}, u32[]{:S(2)}) collective-permute-start(bf16[16,8,512]{2,1,0:T(8,128)(2,1)S(1)} %get-tuple-element.113), channel_id=1, source_target_pairs={{0,252},{4,0},{8,4},{12,8},{16,12},{20,16},{24,20},{28,24},{32,28}... | collective-permute-start | bytes 393224 | tf_op jit(solution)/shard_map/ppermute | solution.py:19
  19.7 1.1 reshape.481
  20.8 1.0 fusion.23
  21.9 21.8 %multiply_bitcast_fusion = f32[16,16,16,16,16]{4,3,2,1,0:T(8,128)} fusion(f32[16,16,16,31]{3,1,0,2:T(8,128)S(1)} %fusion.23, s32[16,16]{1,0:T(8,128)S(1)} %subtract_add_fusion), kind=kOutput, calls=%fused_computation | convolution fusion | flops 394272512 | bytes 4703232 | tf_op jit(solution)/shard_map/csb,hrtb->hrcts/dot_general | solution.py:81
  43.7 23.5 %reshape.485 = f32[16,256,256]{2,1,0:T(8,128)} reshape(f32[16,16,16,16,16]{4,3,2,1,0:T(8,128)} %multiply_bitcast_fusion) | data formatting | bytes 8388608 | tf_op jit(solution)/shard_map/mul | solution.py:82
  67.2 5.3 %copy.60 = f32[16,256,256]{1,2,0:T(8,128)} copy(f32[16,256,256]{2,1,0:T(8,128)} %reshape.485) | data formatting | bytes 8388608 | tf_op jit(solution)/shard_map/mul | solution.py:82
  72.7 1.2 collective-permute-start.1
  73.9 0.8 compare_convert_fusion
  74.8 2.6 collective-permute-done.1
  77.4 1.8 convolution_add_fusion
  79.2 1.9 copy.45
  81.3 6.0 %exponential_multiply_fusion = f32[16,256,256]{1,2,0:T(8,128)S(1)} fusion(f32[16,256,256]{1,2,0:T(8,128)} %copy.60, f32[256,256]{0,1:T(8,128)} %compare_convert_fusion, f32[16]{0:T(128)S(1)} %exp.19, f32[1,256,3,16,32]{1,4,3,2,0:T(8,128)S(1)} %bitcast.154, f32[256,16]{0,1:T(8,128)S(1)} %get-tuple-element.123, f32[256,16]{0,1:T(8,128)S(1)} %get-tuple-element.124), kind=kOutput, calls=%fused_computation.3 | convolution fusion | flops 406061056 | bytes 9732608 | tf_op jit(solution)/shard_map/while/body/eval_jaxpr/wphd,wqhd->whpq/dot_general | solution.py:129
  87.3 2.2 fusion.2
  89.6 0.5 convolution_convert_fusion.2
  90.1 0.9 copy-done.14
  91.0 0.4 fusion.58
  91.9 0.3 copy-done.4
  92.4 10.3 %collective-permute-done.2 = bf16[16,8,512]{2,1,0:T(8,128)(2,1)S(1)} collective-permute-done((bf16[16,8,512]{2,1,0:T(8,128)(2,1)S(1)}, bf16[16,8,512]{2,1,0:T(8,128)(2,1)S(1)}, u32[]{:S(2)}, u32[]{:S(2)}) %collective-permute-start.2) | collective-permute-done | bytes 131104 | tf_op jit(solution)/shard_map/ppermute | solution.py:19
  102.7 0.7 fusion.32
  103.4 1.4 collective-permute-start.3
  104.8 0.6 broadcast_multiply_fusion.1
  105.4 1.3 div.72
  106.7 0.3 collective-permute-done.3
  107.0 1.6 fusion.22
  108.7 1.1 reshape.469
  109.8 0.5 fusion.55
  110.4 3.6 fusion.59
  114.3 0.9 fusion.18
  115.2 1.4 convolution_convert_fusion
  116.8 0.9 copy.48
  117.7 1.7 reshape.472
  119.5 1.0 fusion.53
  120.6 3.8 collective-permute-done.4
  124.4 2.8 collective-permute-start.5
  127.2 2.4 convolution_bitcast_fusion
  129.7 5.4 %copy.66 = f32[256,8,8,128]{3,1,2,0:T(8,128)} copy(f32[256,8,8,128]{3,2,1,0:T(8,128)S(1)} %convolution_bitcast_fusion) | data formatting | bytes 16777216
  135.3 0.6 broadcast_multiply_fusion.2
  136.0 0.6 div.75
  136.7 1.3 multiply_convert_fusion
  138.0 0.7 copy-done.11
  138.7 2.1 convolution_convert_fusion.1
  140.8 1.1 copy.49
  141.9 3.0 convolution_bitcast_fusion.2
  144.9 0.4 copy-done.2
  145.3 0.8 multiply_reduce_fusion
  146.4 1.3 convolution_bitcast_fusion.1
  147.7 4.0 convolution_bitcast_fusion.3
  151.7 2.9 multiply_reduce_fusion.2
  154.6 0.3 multiply_bitcast_fusion.2
  155.0 0.5 copy-done.8
  155.6 2.6 fusion.60
  158.2 4.5 reshape.474
  162.6 1.3 copy.65
  164.0 0.9 copy-done.16
  164.9 0.6 fusion.3
  165.7 10.8 %collective-permute-done.6 = bf16[16,8,512]{2,1,0:T(8,128)(2,1)S(1)} collective-permute-done((bf16[16,8,512]{2,1,0:T(8,128)(2,1)S(1)}, bf16[16,8,512]{2,1,0:T(8,128)(2,1)S(1)}, u32[]{:S(2)}, u32[]{:S(2)}) %collective-permute-start.6) | collective-permute-done | bytes 131104 | tf_op jit(solution)/shard_map/ppermute | solution.py:19
  176.5 2.1 collective-permute-start.7
  178.6 1.9 collective-permute-done.7
  180.5 0.7 fusion.21
  181.2 266.2 %all-reduce.6.cloned.1.call-done = (f32[786432]{0:T(1024)}, f32[262144]{0:T(1024)}, f32[2097152]{0:T(1024)}) async-done(((f32[786432]{0:T(1024)}, f32[262144]{0:T(1024)}, f32[2097152]{0:T(1024)}), (f32[786432]{0:T(1024)}, f32[262144]{0:T(1024)}, f32[2097152]{0:T(1024)})) %all-reduce.6.cloned.1.call-update) | async-done | bytes 12582928
  447.5 1.3 dynamic-slice_multiply_fusion.1
  448.8 1.3 dynamic-slice_multiply_fusion.2
  450.0 1.4 dynamic-slice_multiply_fusion
  (120 shorter events, 2.4 us)
Async XLA Ops:
  7.2 70.3 %copy-start = (bf16[512,1536]{1,0:T(8,128)(2,1)S(1)}, bf16[512,1536]{1,0:T(8,128)(2,1)}, u32[]{:S(2)}) copy-start(bf16[512,1536]{1,0:T(8,128)(2,1)} %param.14) | copy-start | bytes 4718596
  7.2 440.3 %all-reduce.6.cloned.1.call-start = ((), (), s32[]{:S(2)}) async-start(), calls=%async_computation | async-start | bytes 25165824
  8.3 64.4 %collective-permute-start = (bf16[16,8,512]{2,1,0:T(8,128)(2,1)S(1)}, bf16[16,8,512]{2,1,0:T(8,128)(2,1)S(1)}, u32[]{:S(2)}, u32[]{:S(2)}) collective-permute-start(bf16[16,8,512]{2,1,0:T(8,128)(2,1)S(1)} %get-tuple-element.113), channel_id=1, source_target_pairs={{0,252},{4,0},{8,4},{12,8},{16,12},{20,16},{24,20},{28,24},{32,28}... | collective-permute-start | bytes 393224 | tf_op jit(solution)/shard_map/ppermute | solution.py:19
  67.2 5.5 %copy-start.41 = (f32[16]{0:T(128)S(1)}, f32[16]{0:T(128)}, u32[]{:S(2)}) copy-start(f32[16]{0:T(128)} %param.16) | copy-start | bytes 196
  67.2 10.3 %copy-start.31 = (f32[1536]{0:T(1024)S(1)}, f32[1536]{0:T(1024)}, u32[]{:S(2)}) copy-start(f32[1536]{0:T(1024)} %param.15) | copy-start | bytes 18436
  72.7 8.6 %copy-start.33 = (f32[16]{0:T(128)}, f32[16]{0:T(128)S(1)}, u32[]{:S(2)}) copy-start(f32[16]{0:T(128)S(1)} %exp.19) | copy-start | bytes 196
  72.7 4.7 %collective-permute-start.1 = (bf16[8,16,512]{2,1,0:T(8,128)(2,1)S(1)}, bf16[8,16,512]{2,1,0:T(8,128)(2,1)S(1)}, u32[]{:S(2)}, u32[]{:S(2)}) collective-permute-start(bf16[8,16,512]{2,1,0:T(8,128)(2,1)S(1)} %get-tuple-element.111), channel_id=1, source_target_pairs={{0,3},{1,0},{2,1},{3,2},{4,7},{5,4},{6,5},{7,6},{8,11},{9,8},{10,9... | collective-permute-start | bytes 393224 | tf_op jit(solution)/shard_map/ppermute | solution.py:19
  77.4 14.2 %copy-start.7 = (bf16[16,16,512]{2,1,0:T(8,128)(2,1)}, bf16[16,16,512]{2,1,0:T(8,128)(2,1)S(1)}, u32[]{:S(2)}) copy-start(bf16[16,16,512]{2,1,0:T(8,128)(2,1)S(1)} %pad_maximum_fusion.2) | copy-start | bytes 786436
  81.3 6.1 %copy-start.21 = (f32[256,16]{0,1:T(8,128)}, f32[256,16]{0,1:T(8,128)S(1)}, u32[]{:S(2)}) copy-start(f32[256,16]{0,1:T(8,128)S(1)} %get-tuple-element.123) | copy-start | bytes 49156
  89.6 2.4 copy-start.1
  89.6 1.4 copy-start.14
  89.6 1.4 copy-start.38
  89.6 2.1 copy-start.25
  89.6 2.1 copy-start.39
  89.6 2.6 copy-start.13
  89.6 2.6 copy-start.23
  90.1 2.2 copy-start.9
  91.4 0.9 copy-start.4
  91.4 11.3 %copy-start.27 = (f32[256]{0:T(256)}, f32[256]{0:T(256)S(1)}, u32[]{:S(2)}) copy-start(f32[256]{0:T(256)S(1)} %broadcast_multiply_fusion.3) | copy-start | bytes 3076
  91.7 0.6 copy-start.29
  92.2 10.5 %collective-permute-start.2 = (bf16[16,8,512]{2,1,0:T(8,128)(2,1)S(1)}, bf16[16,8,512]{2,1,0:T(8,128)(2,1)S(1)}, u32[]{:S(2)}, u32[]{:S(2)}) collective-permute-start(bf16[16,8,512]{2,1,0:T(8,128)(2,1)S(1)} %get-tuple-element.108), channel_id=1, source_target_pairs={{0,4},{4,8},{8,12},{12,16},{16,20},{20,24},{24,28},{28,32},{32,36}... | collective-permute-start | bytes 393224 | tf_op jit(solution)/shard_map/ppermute | solution.py:19
  103.4 3.6 collective-permute-start.3
  109.7 4.5 copy-start.24
  109.7 4.5 copy-start.37
  109.7 5.5 %copy-start.3 = (bf16[2048,1024]{1,0:T(8,128)(2,1)S(1)}, bf16[2048,1024]{1,0:T(8,128)(2,1)}, u32[]{:S(2)}) copy-start(bf16[2048,1024]{1,0:T(8,128)(2,1)} %param.22) | copy-start | bytes 12582916
  109.8 5.5 %copy-start.36 = (f32[64]{0:T(128)S(1)}, f32[64]{0:T(128)}, u32[]{:S(2)}) copy-start(f32[64]{0:T(128)} %div.72) | copy-start | bytes 772
  110.3 4.8 %copy-start.17 = (bf16[8,1,8,1,512]{4,2,3,1,0:T(8,128)(2,1)}, bf16[8,1,8,1,512]{4,2,3,1,0:T(8,128)(2,1)S(1)}, u32[]{:S(2)}) copy-start(bf16[8,1,8,1,512]{4,2,3,1,0:T(8,128)(2,1)S(1)} %copy.71) | copy-start | bytes 196612
  110.3 4.8 %copy-start.18 = (bf16[8,1,8,1,512]{4,2,3,1,0:T(8,128)(2,1)}, bf16[8,1,8,1,512]{4,2,3,1,0:T(8,128)(2,1)S(1)}, u32[]{:S(2)}) copy-start(bf16[8,1,8,1,512]{4,2,3,1,0:T(8,128)(2,1)S(1)} %copy.72) | copy-start | bytes 196612
  110.4 4.8 %copy-start.19 = (bf16[8,1,8,1,512]{4,2,3,1,0:T(8,128)(2,1)}, bf16[8,1,8,1,512]{4,2,3,1,0:T(8,128)(2,1)S(1)}, u32[]{:S(2)}) copy-start(bf16[8,1,8,1,512]{4,2,3,1,0:T(8,128)(2,1)S(1)} %copy.73) | copy-start | bytes 196612
  110.4 4.8 %copy-start.20 = (bf16[8,1,8,1,512]{4,2,3,1,0:T(8,128)(2,1)}, bf16[8,1,8,1,512]{4,2,3,1,0:T(8,128)(2,1)S(1)}, u32[]{:S(2)}) copy-start(bf16[8,1,8,1,512]{4,2,3,1,0:T(8,128)(2,1)S(1)} %copy.74) | copy-start | bytes 196612
  114.0 2.7 copy-start.32
  114.2 2.5 copy-start.35
  115.2 1.6 copy-start.40
  120.5 3.9 collective-permute-start.4
  124.4 10.7 %collective-permute-start.5 = (bf16[8,16,512]{2,1,0:T(8,128)(2,1)S(1)}, bf16[8,16,512]{2,1,0:T(8,128)(2,1)S(1)}, u32[]{:S(2)}, u32[]{:S(2)}) collective-permute-start(bf16[8,16,512]{2,1,0:T(8,128)(2,1)S(1)} %get-tuple-element.83), channel_id=1, source_target_pairs={{0,3},{1,0},{2,1},{3,2},{4,7},{5,4},{6,5},{7,6},{8,11},{9,8},{10,9... | collective-permute-start | bytes 393224 | tf_op jit(solution)/shard_map/ppermute | solution.py:19
  129.6 5.4 %copy-start.5 = (f32[256,512]{1,0:T(8,128)S(1)}, f32[256,512]{1,0:T(8,128)}, u32[]{:S(2)}) copy-start(f32[256,512]{1,0:T(8,128)} %copy-done.4) | copy-start | bytes 1572868
  129.6 5.4 %copy-start.26 = (f32[512]{0:T(512)S(1)}, f32[512]{0:T(512)}, u32[]{:S(2)}) copy-start(f32[512]{0:T(512)} %param.20) | copy-start | bytes 6148
  129.6 5.4 %copy-start.28 = (f32[256]{0:T(256)S(1)}, f32[256]{0:T(256)}, u32[]{:S(2)}) copy-start(f32[256]{0:T(256)} %copy-done.27) | copy-start | bytes 3076
  129.7 5.4 %copy-start.30 = (f32[256]{0:T(256)S(1)}, f32[256]{0:T(256)}, u32[]{:S(2)}) copy-start(f32[256]{0:T(256)} %copy-done.29) | copy-start | bytes 3076
  135.0 0.8 copy-start.15
  138.0 0.7 copy-start.11
  141.9 3.5 copy-start.2
  145.3 0.9 copy-start.10
  145.3 1.0 copy-start.12
  145.3 2.3 copy-start.34
  147.7 4.0 copy-start.22
  154.6 1.0 copy-start.8
  158.1 4.5 copy-start.6
  164.0 0.9 copy-start.16
  165.6 10.9 %collective-permute-start.6 = (bf16[16,8,512]{2,1,0:T(8,128)(2,1)S(1)}, bf16[16,8,512]{2,1,0:T(8,128)(2,1)S(1)}, u32[]{:S(2)}, u32[]{:S(2)}) collective-permute-start(bf16[16,8,512]{2,1,0:T(8,128)(2,1)S(1)} %get-tuple-element.80), channel_id=1, source_target_pairs={{0,4},{4,8},{8,12},{12,16},{16,20},{20,24},{24,28},{28,32},{32,36}... | collective-permute-start | bytes 393224 | tf_op jit(solution)/shard_map/ppermute | solution.py:19
  176.5 4.0 collective-permute-start.7
Sparse Core Ops, SparseCore 0:
  164.1 283.3 all-reduce.5
where the time goes:
time: 460 us; the launch traced here: 458 us
  waiting for transfers between devices  296 us (64%)
  local copies, waits for them, and re-layouts  56.7 us (12%)
  matrix products  56.2 us (12%)
  starting transfers between devices  19.1 us (4%)
  other arithmetic  15.2 us (3%)
  between operations  14.9 us (3%)
    unnamed x2, waiting for transfers between devices  266 us
    ppermute x8, waiting for transfers between devices, from_behind(): return lax.ppermute(value, axis, pairs)  29.9 us
    mul x2, local copies, waits for them, and re-layouts, bias_from_table(): 16.0 * jax.nn.sigmoid(full.reshape(head_count, window * window, window *...  28.8 us
    dot_general x1, matrix products, bias_from_table(): full = jnp.einsum('csb,hrtb->hrcts', onehot, by_rows, precision=HIGH)  21.8 us
    ppermute x8, starting transfers between devices, from_behind(): return lax.ppermute(value, axis, pairs)  19 us
    unnamed x90, local copies, waits for them, and re-layouts  10.9 us
  transfers between devices with their start and end apart: 9, of which 7 were waited for; matrix products, arithmetic and copies ran while one was open for 14% of the time, Pallas kernels for 0%

commit v1 on v0

v1 whole, which is shorter than its diff:
```python
import functools
import math

import jax
import jax.numpy as jnp
from jax import lax
from jax.experimental import pallas as pl
from jax.experimental.pallas import tpu as pltpu
from jax.sharding import PartitionSpec as P

MESH = pl.DeviceIdType.MESH
F32 = jnp.float32
BF16 = jnp.bfloat16

CH = 512
HEADS = 16
HEAD = 32
TOK = 256
MTOK = 64
WIDE = 1024
EPS_NORM = 1e-05
EPS_COS = 1e-06
LOG2E = math.log2(math.e)
LN2 = math.log(2.0)

NN = (((1,), (0,)), ((), ()))
NT = (((1,), (1,)), ((), ()))
TN = (((0,), (0,)), ((), ()))


def mm(left, right, dims=NN):
    return lax.dot_general(left, right, dims, preferred_element_type=F32)


def iotas(shape):
    return (
        lax.broadcasted_iota(jnp.int32, shape, 0),
        lax.broadcasted_iota(jnp.int32, shape, 1),
    )


def onehot(cond):
    return jnp.where(cond, 1.0, 0.0).astype(BF16)


def quad_source(t):
    quad, a, b = t >> 6, (t >> 3) & 7, t & 7
    return ((quad >> 1) * 8 + a) * 16 + (quad & 1) * 8 + b


def group_source(t):
    member, quad, i, j = t >> 6, (t >> 4) & 3, (t >> 2) & 3, t & 3
    row = (quad >> 1) * 8 + 2 * i + (member & 1)
    col = (quad & 1) * 8 + 2 * j + (member >> 1)
    return row * 16 + col


def merged_source(u):
    quad, i, j = u >> 4, (u >> 2) & 3, u & 3
    return ((quad >> 1) * 4 + i) * 8 + (quad & 1) * 4 + j


def channel_source(t):
    core, parity = t >> 8, (t >> 7) & 1
    x, y, z = (t >> 5) & 3, (t >> 3) & 3, t & 7
    owner = (x >> 1) * 128 + z * 16 + y * 4 + (x & 1) * 2 + core
    return 2 * owner + parity


class Place:
    def __init__(self):
        self.c = lax.axis_index("cols")
        self.r = lax.axis_index("rows")
        self.x = (self.c // 32) * 2 + self.r // 2
        self.z = (self.c // 4) % 8
        self.y = self.c % 4
        self.k = self.r % 2
        self.coord = {"x": self.x, "y": self.y, "z": self.z}

    def beside(self, dc, dr):
        return ((self.c + dc + 64) % 64, (self.r + dr + 4) % 4)

    def sibling(self):
        return (self.c, self.r + 1 - 2 * self.k)

    def along(self, axis, step, core=None):
        core = self.k if core is None else core
        at = dict(self.coord)
        size = AXES[axis]
        at[axis] = (at[axis] + step + size) % size
        return ((at["x"] // 2) * 32 + at["z"] * 4 + at["y"], (at["x"] % 2) * 2 + core)


OPERANDS = (
    "image", "gout", "wq_in", "wp_in", "wm_in", "bq", "ls", "tab", "bp", "ga", "sa", "gm", "sm"
)
LOADS = (("image", "tile"), ("gout", "gtile"), ("wq_in", "wq"), ("wp_in", "wp"), ("wm_in", "wm"))
RESULTS = ("merged", "gimage", "gqkv", "gproj", "gmerge")
AXES = {"x": 4, "y": 4, "z": 8}
ORDERS = (("x", "y"), ("y", "x"))

SCRATCH = {
    "wq": ((CH, 3 * CH), BF16),
    "wp": ((CH, CH), BF16),
    "wm": ((4 * CH, WIDE), BF16),
    "wqT": ((3 * CH, CH), BF16),
    "wpT": ((CH, CH), BF16),
    "sentX": ((4, 64, CH), BF16),
    "gotX": ((4, 64, CH), BF16),
    "sentG": ((4, 16, WIDE), BF16),
    "gotG": ((4, 16, WIDE), BF16),
    "sentO": ((4, 16, WIDE), BF16),
    "gotO": ((4, 16, WIDE), BF16),
    "sentI": ((4, 64, CH), BF16),
    "gotI": ((4, 64, CH), BF16),
    "table": ((HEADS, 1024), F32),
    "bias": ((HEADS, TOK, TOK), F32),
    "colq": ((3 * CH, 128), F32),
    "colp": ((CH, 128), F32),
    "colg": ((CH, 128), F32),
    "cols": ((CH, 128), F32),
    "xT": ((CH, TOK), BF16),
    "qs": ((CH, TOK), BF16),
    "qu": ((CH, TOK), F32),
    "ku": ((CH, TOK), F32),
    "kb": ((CH, TOK), BF16),
    "vb": ((CH, TOK), BF16),
    "qinv": ((HEADS, TOK), F32),
    "kinv": ((HEADS, TOK), F32),
    "linv": ((HEADS, TOK), F32),
    "soft": ((HEADS, TOK, TOK), BF16),
    "att": ((CH, TOK), BF16),
    "normed": ((CH, TOK), F32),
    "dA": ((CH, TOK), BF16),
    "upT": ((CH, TOK), F32),
    "rows": ((2, TOK, TOK), BF16),
    "rowsGot": ((TOK, TOK), BF16),
    "attP": ((2, TOK, TOK), BF16),
    "attGot": ((TOK, TOK), BF16),
    "dproj": ((CH, TOK), BF16),
    "dprojGot": ((CH, TOK), BF16),
    "dmix": ((2, 3 * TOK, TOK), BF16),
    "dmixGot": ((2, 3 * TOK, TOK), BF16),
    "tile": ((TOK, CH), BF16),
    "gtile": ((MTOK, WIDE), BF16),
    "gath": ((4, 2, MTOK, 256), BF16),
    "gathAll": ((8, MTOK, 256), BF16),
    "dredAll": ((8, MTOK, WIDE), BF16),
    "ms1": ((4, 8, 16, 512), BF16),
    "mr1": ((3, 8, 16, 512), BF16),
    "ms2": ((8, 16, 512), BF16),
    "mr2": ((7, 16, 512), BF16),
    "qs1": ((2, 2, 4, 4, 4, 16, 128), BF16),
    "qr1": ((2, 2, 3, 4, 4, 16, 128), BF16),
    "qs2": ((2, 2, 4, 4, 16, 128), BF16),
    "qr2": ((2, 2, 3, 4, 16, 128), BF16),
    "qs3": ((2, 8, 16, 128), BF16),
    "qr3": ((2, 7, 16, 128), BF16),
    "fold0": ((128 * 16, 128), F32),
    "fold1": ((128 * 16, 128), F32),
}
COPIES = 96


def kernel(factor, *refs):
    names = OPERANDS + RESULTS + tuple(SCRATCH) + ("ssem", "rsem", "lsem")
    ref = dict(zip(names, refs, strict=True))
    place = Place()
    used = [0]
    pending = []

    def send(src, dst, device):
        index = used[0]
        used[0] += 1
        copy = pltpu.make_async_remote_copy(
            src_ref=src,
            dst_ref=dst,
            send_sem=ref["ssem"].at[index],
            recv_sem=ref["rsem"].at[index],
            device_id=device,
            device_id_type=MESH,
        )
        copy.start()
        pending.append(copy)
        return copy

    partners = [(dc, dr) for dc in (-1, 0, 1) for dr in (-1, 0, 1) if dc * dr >= 0 and (dc, dr) != (0, 0)]
    greeted = [place.beside(dc, dr) for dc, dr in partners] + [place.sibling()]
    for axis, size in AXES.items():
        greeted += [place.along(axis, step) for step in range(1, size)]
    greeted += [place.along("x", step, 1 - place.k) for step in range(1, 4)]
    barrier = pltpu.get_barrier_semaphore()
    for device in greeted:
        pl.semaphore_signal(barrier, inc=1, device_id=device, device_id_type=MESH)

    loads = {}
    for index, (src, dst) in enumerate(LOADS):
        loads[dst] = pltpu.make_async_copy(ref[src], ref[dst], ref["lsem"].at[index])
        loads[dst].start()

    t, n = iotas((TOK, TOK))
    to_quads = onehot(n == quad_source(t))
    from_quads = onehot(t == quad_source(n))
    groups = onehot(n == group_source(t))
    u, v = iotas((MTOK, MTOK))
    merged_quads = onehot(v == merged_source(u))
    merged_back = onehot(u == merged_source(v))
    loads["tile"].wait()
    ref["sentX"][...] = mm(to_quads, ref["tile"][...]).astype(BF16).reshape(4, 64, CH)
    loads["gtile"].wait()
    ref["sentG"][...] = mm(merged_quads, ref["gtile"][...]).astype(BF16).reshape(4, 16, WIDE)
    pl.semaphore_wait(barrier, len(greeted))

    def to_window(sent, got):
        copies = []
        for quad in (2, 1, 0):
            rh, ch = quad >> 1, quad & 1
            copies.append(
                send(ref[sent].at[quad], ref[got].at[3 - quad], place.beside(ch - 1, rh - 1))
            )
        ref[got][0] = ref[sent][3]
        return copies

    def to_image(sent, got):
        copies = []
        for quad in (3, 2, 1):
            qr, qc = quad >> 1, quad & 1
            copies.append(send(ref[sent].at[quad], ref[got].at[3 - quad], place.beside(qc, qr)))
        ref[got][3] = ref[sent][0]
        return copies

    came_x = to_window("sentX", "gotX")
    came_g = to_window("sentG", "gotG")

    def column(src, dst, size):
        ref[dst][...] = jnp.broadcast_to(ref[src][...].reshape(1, size), (128, size)).T

    column("bq", "colq", 3 * CH)
    column("bp", "colp", CH)
    column("ga", "colg", CH)
    column("sa", "cols", CH)

    def wide(name, rows=slice(None)):
        col = ref[name][rows, :]
        return jnp.concatenate([col, col], axis=1)

    build_bias(ref, place)
    loads["wq"].wait()
    loads["wp"].wait()
    for part in range(3):
        ref["wqT"][part * CH : (part + 1) * CH, :] = ref["wq"][:, part * CH : (part + 1) * CH].T
    ref["wpT"][...] = ref["wp"][...].T

    for copy in came_x:
        copy.wait_recv()
    x = mm(from_quads, ref["gotX"][...].reshape(TOK, CH)).astype(BF16)
    q = mm(ref["wqT"][:CH, :], x, NT) + wide("colq", slice(0, CH))
    k = mm(ref["wqT"][CH : 2 * CH, :], x, NT) + wide("colq", slice(CH, 2 * CH))
    val = mm(ref["wqT"][2 * CH :, :], x, NT) + wide("colq", slice(2 * CH, 3 * CH))
    ref["vb"][...] = val.astype(BF16)
    q = q.reshape(HEADS, HEAD, TOK)
    k = k.reshape(HEADS, HEAD, TOK)
    qinv = lax.rsqrt(jnp.sum(q * q, axis=1, keepdims=True) + EPS_COS)
    kinv = lax.rsqrt(jnp.sum(k * k, axis=1, keepdims=True) + EPS_COS)
    qu = (q * qinv).reshape(CH, TOK)
    ku = (k * kinv).reshape(CH, TOK)
    ref["qinv"][...] = qinv.reshape(HEADS, TOK)
    ref["kinv"][...] = kinv.reshape(HEADS, TOK)
    ref["qu"][...] = qu
    ref["ku"][...] = ku
    ref["kb"][...] = ku.astype(BF16)

    def scale_of(h):
        return jnp.exp(jnp.full((1, TOK), ref["ls"][h], F32))

    for h in range(HEADS):
        at = slice(h * HEAD, (h + 1) * HEAD)
        ref["qs"][at, :] = (qu[at, :] * (scale_of(h) * LOG2E)).astype(BF16)
    ref["xT"][...] = x.astype(F32).T.astype(BF16)

    a, b = iotas((CH, CH))
    owners = onehot(b == channel_source(a))
    ref["rows"][...] = mm(owners, x, NT).astype(BF16).reshape(2, TOK, TOK)
    came_rows = send(ref["rows"].at[1 - place.k], ref["rowsGot"], place.sibling())

    def attend(h):
        at = pl.ds(pl.multiple_of(h * HEAD, HEAD), HEAD)
        raised = jnp.exp2(mm(ref["kb"][at, :], ref["qs"][at, :], TN)) * ref["bias"][h]
        total = jnp.sum(raised, axis=0, keepdims=True)
        low = raised.astype(BF16)
        ref["soft"][h] = low
        inverse = 1.0 / total
        ref["linv"][pl.ds(h, 1), :] = inverse
        ref["att"][at, :] = (mm(ref["vb"][at, :], low) * inverse).astype(BF16)

    @pl.loop(0, HEADS // 4)
    def _(group):
        for inner in range(4):
            attend(group * 4 + inner)

    att = ref["att"][...]
    projected = mm(ref["wpT"][...], att) + wide("colp")
    average = jnp.mean(projected, axis=0, keepdims=True)
    centered = projected - average
    inverse = lax.rsqrt(jnp.mean(centered * centered, axis=0, keepdims=True) + EPS_NORM)
    normed = centered * inverse
    ref["normed"][...] = normed
    gain = wide("colg")
    branch = ref["xT"][...].astype(F32) + normed * gain + wide("cols")
    result = branch.astype(BF16)

    blocks = branch.reshape(16, 4, 8, TOK)
    ordered = jnp.concatenate([blocks[:, owner].reshape(128, TOK) for owner in range(4)], axis=0)
    ordered = ordered.astype(BF16)
    for member in range(4):
        pick = groups[member * 64 : (member + 1) * 64, :]
        part = mm(pick, ordered, NT).astype(BF16)
        lanes = slice((member & 1) * 128, (member & 1) * 128 + 128)
        for owner in range(4):
            x, core = (member >> 1) * 2 + (owner >> 1), owner & 1
            ref["gath"][x, core, :, lanes] = part[:, owner * 128 : (owner + 1) * 128]
    came_tokens = []
    ref["gathAll"][place.k] = ref["gath"][place.x, place.k]
    for step in (2, 1, 3, 0):
        for other in range(2):
            if step or other:
                core = place.k + other - 2 * other * place.k
                x = (place.x + step) % 4
                device = place.along("x", step, core)
                slot = 2 * step + place.k
                came_tokens.append(send(ref["gath"].at[x, core], ref["gathAll"].at[slot], device))
    loads["wm"].wait()
    reduced = None
    for member in range(4):
        pick = groups[member * 64 : (member + 1) * 64, :]
        gathered = mm(pick, result, NT).astype(BF16)
        term = mm(gathered, ref["wm"][member * CH : (member + 1) * CH, :])
        reduced = term if reduced is None else reduced + term
    m_average = jnp.mean(reduced, axis=-1, keepdims=True)
    m_centered = reduced - m_average
    m_inverse = lax.rsqrt(jnp.mean(m_centered * m_centered, axis=-1, keepdims=True) + EPS_NORM)
    m_normed = m_centered * m_inverse
    merged = m_normed * ref["gm"][...] + ref["sm"][...]
    ref["sentO"][...] = merged.astype(BF16).reshape(4, 16, WIDE)
    for copy in came_g:
        copy.wait_recv()
    came_o = to_image("sentO", "gotO")
    scaled = ref["gotG"][...].reshape(MTOK, WIDE).astype(F32) * ref["gm"][...]
    m_mean = jnp.mean(scaled, axis=-1, keepdims=True)
    m_proj = jnp.mean(scaled * m_normed, axis=-1, keepdims=True)
    d_reduced = (m_inverse * (scaled - m_mean - m_normed * m_proj)).astype(BF16)
    ref["dredAll"][place.k] = d_reduced
    own = ref["dredAll"].at[place.k]
    came_dred = {}
    for step in (2, 1, 3):
        slot = 2 * step + place.k
        came_dred[step] = send(own, ref["dredAll"].at[slot], place.along("x", step))
    came_tokens.append(send(own, own, place.sibling()))

    def pass_on(step):
        came_dred[step].wait_recv()
        slot = ref["dredAll"].at[2 * step + place.k]
        came_tokens.append(send(slot, slot, place.sibling()))

    upstream = None
    for member in range(4):
        d_in = mm(ref["wm"][member * CH : (member + 1) * CH, :], d_reduced, NT).astype(BF16)
        term = mm(d_in, groups[member * 64 : (member + 1) * 64, :])
        upstream = term if upstream is None else upstream + term
    ref["upT"][...] = upstream
    a_scaled = upstream * gain
    a_mean = jnp.mean(a_scaled, axis=0, keepdims=True)
    a_proj = jnp.mean(a_scaled * normed, axis=0, keepdims=True)
    ref["dproj"][...] = (inverse * (a_scaled - a_mean - normed * a_proj)).astype(BF16)
    came_dproj = send(ref["dproj"], ref["dprojGot"], place.sibling())
    ref["attP"][...] = mm(owners, att).astype(BF16).reshape(2, TOK, TOK)
    came_att = send(ref["attP"].at[1 - place.k], ref["attGot"], place.sibling())

    def start_stage(src, dst, axis):
        mine, size = place.coord[axis], AXES[axis]
        copies = []
        for step in range(1, size):
            slot = dst.at[step - 1]
            copies.append(send(src.at[(mine + step) % size], slot, place.along(axis, step)))
        return copies

    def end_stage(src, dst, axis, copies):
        total = src[place.coord[axis]].astype(F32)
        for step, copy in enumerate(copies):
            copy.wait_recv()
            total = total + dst[step].astype(F32)
        return total

    def q_refs(half, zh, stage):
        if stage == 2:
            return ref["qs3"].at[half], ref["qr3"].at[half]
        number = str(stage + 1)
        return ref["qs" + number].at[half, zh], ref["qr" + number].at[half, zh]

    def start_q(half, stage):
        if stage == 2:
            return [start_stage(*q_refs(half, 0, 2), "z")]
        return [start_stage(*q_refs(half, zh, stage), ORDERS[zh][stage]) for zh in range(2)]

    def end_q(half, stage):
        for zh in range(2):
            total = end_stage(*q_refs(half, zh, stage), ORDERS[zh][stage], q_stage[half][zh])
            if stage == 0:
                ref["qs2"][half, zh] = total.astype(BF16)
            else:
                ref["qs3"][half, 4 * zh : 4 * zh + 4] = total.astype(BF16)

    q_stage = []

    d_attended = mm(ref["wp"][...], ref["dproj"][...]).astype(BF16)
    ref["dA"][...] = d_attended

    def attend_back(h):
        at = pl.ds(pl.multiple_of(h * HEAD, HEAD), HEAD)
        linv = ref["linv"][pl.ds(h, 1), :]
        d_att = ref["dA"][at, :].astype(F32) * linv
        delta = jnp.sum(d_att * ref["att"][at, :].astype(F32), axis=0, keepdims=True)
        d_low = d_att.astype(BF16)
        soft = ref["soft"][h]
        d_soft = mm(ref["vb"][at, :], d_low, TN)
        d_scores = (soft.astype(F32) * (d_soft - delta)).astype(BF16)
        scale = scale_of(h)
        d_value = mm(d_low, soft, NT)
        d_qu = mm(ref["kb"][at, :], d_scores) * scale
        d_ku = mm(ref["qs"][at, :], d_scores, NT) * LN2
        q_unit, k_unit = ref["qu"][at, :], ref["ku"][at, :]
        d_q = ref["qinv"][pl.ds(h, 1), :] * (
            d_qu - q_unit * jnp.sum(q_unit * d_qu, axis=0, keepdims=True)
        )
        d_k = ref["kinv"][pl.ds(h, 1), :] * (
            d_ku - k_unit * jnp.sum(k_unit * d_ku, axis=0, keepdims=True)
        )
        for part, values in enumerate((d_q, d_k, d_value)):
            rows = pl.ds(pl.multiple_of(part * 256 + (h & 7) * HEAD, HEAD), HEAD)
            ref["dmix"][h >> 3, rows, :] = values.astype(BF16)

    folds = (ref["fold0"], ref["fold1"])

    def put(half, unit, values):
        for lane in range(2):
            part = values[:, lane * 128 : (lane + 1) * 128]
            folds[half][pl.ds(unit + lane, 128, stride=16), :] = part

    came_mix = []
    for half in range(2):

        @pl.loop(half * 2, half * 2 + 2)
        def _(group):
            for inner in range(4):
                attend_back(group * 4 + inner)

        came_mix.append(send(ref["dmix"].at[half], ref["dmixGot"].at[half], place.sibling()))
        if half == 0:
            pass_on(1)
            pass_on(3)
            came_rows.wait_recv()
            came_att.wait_recv()
            came_dproj.wait_recv()
            own_att = ref["attP"][place.k]
            for piece in range(2):
                cols = slice(piece * 256, (piece + 1) * 256)
                part = mm(own_att, ref["dproj"][cols, :], NT)
                part = part + mm(ref["attGot"][...], ref["dprojGot"][cols, :], NT)
                put(0, 12 + 2 * piece, part[:128])
                put(1, 12 + 2 * piece, part[128:])
        else:
            pass_on(2)
            d_rows = None
            for block in range(6):
                cols = slice((block % 3) * 512 + (block // 3) * 256, (block % 3) * 512 + (block // 3) * 256 + 256)
                rows = slice((block % 3) * 256, (block % 3) * 256 + 256)
                term = mm(ref["wq"][:, cols], ref["dmix"][block // 3, rows, :])
                d_rows = term if d_rows is None else d_rows + term
            d_image = (ref["upT"][...] + d_rows).astype(BF16)
            ref["sentI"][...] = mm(to_quads, d_image, NT).astype(BF16).reshape(4, 64, CH)
            came_i = to_image("sentI", "gotI")
        came_mix[half].wait_recv()
        own_rows = ref["rows"][place.k]
        for part in range(3):
            cols = slice(part * 256, (part + 1) * 256)
            values = mm(own_rows, ref["dmix"][half, cols, :], NT)
            values = values + mm(ref["rowsGot"][...], ref["dmixGot"][half, cols, :], NT)
            put(half, 2 * part, values[:128])
            put(half, 6 + 2 * part, values[128:])
        for first in range(4):
            for second in range(4):
                at = pl.ds((first * 4 + second) * 128, 128)
                share = folds[half][at, :].astype(BF16).reshape(8, 16, 128)
                ref["qs1"][half, 0, first, second] = share[:4]
                ref["qs1"][half, 1, second, first] = share[4:]
        q_stage.append(start_q(half, 0))
    for copy in came_tokens:
        copy.wait_recv()
    tokens = ref["gathAll"][...].reshape(8 * MTOK, 256)
    grads = mm(tokens, ref["dredAll"][...].reshape(8 * MTOK, WIDE), TN).reshape(8, 4, 8, WIDE)
    shares = jnp.concatenate([grads[..., :512], grads[..., 512:]], axis=2).astype(BF16)
    for y in range(4):
        ref["ms1"][y] = shares[:, y]
    m_copies = start_stage(ref["ms1"], ref["mr1"], "y")

    end_q(0, 0)
    q_stage[0] = start_q(0, 1)
    end_q(1, 0)
    q_stage[1] = start_q(1, 1)

    for copy in came_o:
        copy.wait_recv()
    ref["merged"][...] = mm(merged_back, ref["gotO"][...].reshape(MTOK, WIDE)).astype(BF16)

    end_q(0, 1)
    q_stage[0] = start_q(0, 2)
    end_q(1, 1)
    q_stage[1] = start_q(1, 2)
    ref["ms2"][...] = end_stage(ref["ms1"], ref["mr1"], "y", m_copies).astype(BF16)
    m_copies = start_stage(ref["ms2"], ref["mr2"], "z")

    for copy in came_i:
        copy.wait_recv()
    ref["gimage"][...] = mm(from_quads, ref["gotI"][...].reshape(TOK, CH)).astype(BF16)

    for half in range(2):
        total = end_stage(*q_refs(half, 0, 2), "z", q_stage[half][0]) * factor
        for parity in range(2):
            for part in range(3):
                row, unit = parity * 12 + part * 4 + half * 2, parity * 6 + part * 2
                ref["gqkv"][row : row + 2, :] = total[unit : unit + 2]
        ref["gproj"][half * 4 : half * 4 + 4, :] = total[12:]
    total = end_stage(ref["ms2"], ref["mr2"], "z", m_copies) * factor
    for fold in range(2):
        for lane in range(4):
            part = total[fold * 8 : fold * 8 + 8, lane * 128 : (lane + 1) * 128]
            ref["gmerge"][pl.ds(fold * 4 + lane, 8, stride=8), :] = part
    for copy in pending:
        copy.wait_send()
    assert used[0] <= COPIES


def build_bias(ref, place):
    ref["table"][...] = jnp.zeros((HEADS, 1024), F32)
    ref["table"][:, :961] = (16.0 * LOG2E) * jax.nn.sigmoid(ref["tab"][...])
    high = ref["table"][...].astype(BF16).astype(F32)
    low = ref["table"][...] - high
    k = lax.broadcasted_iota(jnp.int32, (HEAD, 1024), 1)
    b = lax.broadcasted_iota(jnp.int32, (HEAD, 1024), 0)
    chosen = jnp.where((k - 31 * ((k * 2115) >> 16)) == 30 - b, 1.0, 0.0)
    k, lane = iotas((1024, 512))
    spread = onehot(((k * 2115) >> 16) == (lane >> 4))
    terms = None
    for part in (high, low):
        left = (part[:, None, :] * chosen[None]).reshape(HEADS * HEAD, 1024).astype(BF16)
        term = mm(left, spread)
        terms = term if terms is None else terms + term
    lane = lax.broadcasted_iota(jnp.int32, (HEAD, 512), 1)
    shift = 15 - (lane & 15)
    q, p = iotas((TOK, TOK))
    last_row = place.r == 3
    last_col = place.c == 63
    row_cut = jnp.where((q >> 7) != (p >> 7), jnp.where(last_row, 0.0, 1.0), 1.0)
    col_cut = jnp.where(((q >> 3) & 1) != ((p >> 3) & 1), jnp.where(last_col, 0.0, 1.0), 1.0)
    allowed = row_cut * col_cut
    for h in range(HEADS):
        rows = terms[h * HEAD : (h + 1) * HEAD, :]
        for bit in range(4):
            moved = pltpu.roll(rows, HEAD - (1 << bit), 0)
            rows = jnp.where(((shift >> bit) & 1) == 1, moved, rows)
        rows = jnp.exp2(rows[:16])
        for turn in range(8):
            turned = rows if turn == 0 else pltpu.roll(rows, 512 - 16 * turn, 1)
            for whole in range(2):
                row = 15 - (whole * 8 + turn)
                at = slice(row * 16, (row + 1) * 16)
                ref["bias"][h, at, :] = turned[:, whole * 128 : whole * 128 + 256] * allowed[at, :]


def copy_out(*refs):
    count = len(refs) // 2
    for index in range(count):
        refs[count + index][...] = refs[index][...]


def hand_over(arrays):
    vmem = pl.BlockSpec(memory_space=pltpu.VMEM)
    return pl.pallas_call(
        copy_out,
        name="results",
        out_shape=tuple(jax.ShapeDtypeStruct(a.shape, a.dtype) for a in arrays),
        in_specs=[vmem] * len(arrays),
        out_specs=(vmem,) * len(arrays),
    )(*arrays)


def per_device(
    image,
    w_qkv,
    b_qkv,
    logit_scale,
    bias_table,
    w_proj,
    b_proj,
    gain_attn,
    shift_attn,
    w_merge,
    gain_merge,
    shift_merge,
    grad_out,
):
    vmem = pl.BlockSpec(memory_space=pltpu.VMEM)
    smem = pl.BlockSpec(memory_space=pltpu.SMEM)
    anywhere = pl.BlockSpec(memory_space=pl.ANY)
    factor = 1.0 / math.sqrt(16384)
    outs = pl.pallas_call(
        functools.partial(kernel, factor),
        name="block",
        out_shape=(
            jax.ShapeDtypeStruct((MTOK, WIDE), BF16),
            jax.ShapeDtypeStruct((TOK, CH), BF16),
            jax.ShapeDtypeStruct((24, 128), F32),
            jax.ShapeDtypeStruct((8, 128), F32),
            jax.ShapeDtypeStruct((64, 128), F32),
        ),
        in_specs=[anywhere] * 5 + [vmem, smem] + [vmem] * 6,
        out_specs=(vmem,) * 5,
        scratch_shapes=[pltpu.VMEM(shape, dtype) for shape, dtype in SCRATCH.values()]
        + [
            pltpu.SemaphoreType.DMA((COPIES,)),
            pltpu.SemaphoreType.DMA((COPIES,)),
            pltpu.SemaphoreType.DMA((len(LOADS),)),
        ],
        compiler_params=pltpu.CompilerParams(
            collective_id=0, has_side_effects=True, vmem_limit_bytes=60 * 2**20
        ),
    )(
        image.reshape(TOK, CH),
        grad_out.reshape(MTOK, WIDE),
        w_qkv,
        w_proj,
        w_merge,
        b_qkv,
        logit_scale,
        bias_table,
        b_proj.reshape(1, -1),
        gain_attn.reshape(1, -1),
        shift_attn.reshape(1, -1),
        gain_merge.reshape(1, -1),
        shift_merge.reshape(1, -1),
    )
    merged, gimage, gqkv, gproj, gmerge = hand_over(outs)
    return (
        merged.reshape(8, 8, WIDE),
        gimage.reshape(16, 16, CH),
        gqkv.reshape(-1),
        gproj.reshape(-1),
        gmerge.reshape(-1),
    )


def solution(mesh):
    whole = P()
    tiles = P("rows", "cols", None)
    flat = P(("cols", "rows"))
    return jax.shard_map(
        per_device,
        mesh=mesh,
        in_specs=(tiles,) + (whole,) * 11 + (tiles,),
        out_specs=(tiles, tiles, flat, flat, flat),
        check_vma=False,
    )
```

time: 460 us -> 66.1 us (0.14)
  waiting for transfers between devices: 296 us -> 0 us
  Pallas kernels: 0 us -> 65.3 us
  local copies, waits for them, and re-layouts: 56.7 us -> 0 us
  matrix products: 56.2 us -> 0 us
  starting transfers between devices: 19.1 us -> 0 us
  other arithmetic: 15.2 us -> 0 us
  between operations: 14.9 us -> 0.65 us
    unnamed x2 -> x0, waiting for transfers between devices: 266 us -> none
    pallas_call x0 -> x2, Pallas kernels: none -> 65.3 us  [the longest x1 63.5 us: per_device(): pl.pallas_call(functools.partial(kernel, factor), name='block', out_shape...]
    dot_general x17 -> x0, matrix products: 56.2 us -> none  [the longest x1 21.8 us: bias_from_table(): full = jnp.einsum('csb,hrtb->hrcts', onehot, by_rows, precision=HIGH)]
    ppermute x8 -> x0, waiting for transfers between devices: 29.9 us -> none  [from_behind(): return lax.ppermute(value, axis, pairs)]
    mul x2 -> x0, local copies, waits for them, and re-layouts: 28.8 us -> none  [bias_from_table(): 16.0 * jax.nn.sigmoid(full.reshape(head_count, window * window, window *...]
    ppermute x8 -> x0, starting transfers between devices: 19 us -> none  [from_behind(): return lax.ppermute(value, axis, pairs)]
    unnamed x90 -> x0, local copies, waits for them, and re-layouts: 10.9 us -> none
    reshape x4 -> x0, local copies, waits for them, and re-layouts: 8.37 us -> none  [the longest x1 4.46 us: per_device(): grads[0].reshape(-1)]
  transfers between devices with their start and end apart: 9 -> 0, of which waited for: 7 -> 0; matrix products, arithmetic and copies ran while one was open for 14% -> 0% of each run, Pallas kernels for 0% -> 0%
where the time goes in v1:
time: 66.1 us; the launch traced here: 65.9 us
  Pallas kernels  65.3 us (99%)
    pallas_call x1, Pallas kernels, per_device(): pl.pallas_call(functools.partial(kernel, factor), name='block', out_shape...  63.5 us
    pallas_call x1, Pallas kernels, hand_over(): pl.pallas_call(copy_out, name='results', out_shape=tuple((jax.ShapeDtypeS...  1.76 us

profile of v1, /device:TPU:1, one launch (start us, length us, event | category | flops | bytes accessed | tf_op | source)
XLA Modules:
  0.0 65.9 jit_solution(6623513242064591387)
XLA Ops:
  0.6 63.5 %block.1 = (bf16[64,1024]{1,0:T(8,128)(2,1)}, bf16[256,512]{1,0:T(8,128)(2,1)}, f32[24,128]{1,0:T(8,128)}, f32[8,128]{1,0:T(8,128)}, f32[64,128]{1,0:T(8,128)}) custom-call(bf16[256,512]{1,0:T(8,128)(2,1)} %bitcast.12, bf16[64,1024]{1,0:T(8,128)(2,1)} %bitcast.13, bf16[512,1536]{1,0:T(8,128)(2,1)} %refs_2_.1, bf16[512,512]{1,0:T(8,128)(2,1)} %refs_3_.1, ...), custom_call_target="tpu_custom_call" | custom-call | tf_op jit(solution)/shard_map/block/pallas_call | solution.py:616
  64.2 1.8 %results.1 = (bf16[64,1024]{1,0:T(8,128)(2,1)}, bf16[256,512]{1,0:T(8,128)(2,1)}, f32[24,128]{1,0:T(8,128)}, f32[8,128]{1,0:T(8,128)}, f32[64,128]{1,0:T(8,128)}) custom-call(bf16[64,1024]{1,0:T(8,128)(2,1)} %get-tuple-element.15.refs_0_, bf16[256,512]{1,0:T(8,128)(2,1)} %get-tuple-element.16.refs_1_, f32[24,128]{1,0:T(8,128)} %get-tuple-element.17.refs_2_, ...), custom_call_target="tpu_custom_call" | custom-call | tf_op jit(solution)/shard_map/results/pallas_call | solution.py:588

commit v2 on v1

--- a/solution.py
+++ b/solution.py
@@ -145,11 +145,11 @@
     "gtile": ((MTOK, WIDE), BF16),
     "gath": ((4, 2, MTOK, 256), BF16),
     "gathAll": ((8, MTOK, 256), BF16),
-    "dredAll": ((8, MTOK, WIDE), BF16),
-    "ms1": ((4, 8, 16, 512), BF16),
-    "mr1": ((3, 8, 16, 512), BF16),
-    "ms2": ((8, 16, 512), BF16),
-    "mr2": ((7, 16, 512), BF16),
+    "dredAll": ((2, 8, MTOK, CH), BF16),
+    "ms1": ((2, 4, 8, 16, 256), BF16),
+    "mr1": ((2, 3, 8, 16, 256), BF16),
+    "ms2": ((2, 8, 16, 256), BF16),
+    "mr2": ((2, 7, 16, 256), BF16),
     "qs1": ((2, 2, 4, 4, 4, 16, 128), BF16),
     "qr1": ((2, 2, 3, 4, 4, 16, 128), BF16),
     "qs2": ((2, 2, 4, 4, 16, 128), BF16),
@@ -293,10 +293,8 @@
         ref["linv"][pl.ds(h, 1), :] = inverse
         ref["att"][at, :] = (mm(ref["vb"][at, :], low) * inverse).astype(BF16)
 
-    @pl.loop(0, HEADS // 4)
-    def _(group):
-        for inner in range(4):
-            attend(group * 4 + inner)
+    for h in range(HEADS):
+        attend(h)
 
     att = ref["att"][...]
     projected = mm(ref["wpT"][...], att) + wide("colp")
@@ -349,24 +347,40 @@
     m_mean = jnp.mean(scaled, axis=-1, keepdims=True)
     m_proj = jnp.mean(scaled * m_normed, axis=-1, keepdims=True)
     d_reduced = (m_inverse * (scaled - m_mean - m_normed * m_proj)).astype(BF16)
-    ref["dredAll"][place.k] = d_reduced
-    own = ref["dredAll"].at[place.k]
     came_dred = {}
-    for step in (2, 1, 3):
-        slot = 2 * step + place.k
-        came_dred[step] = send(own, ref["dredAll"].at[slot], place.along("x", step))
-    came_tokens.append(send(own, own, place.sibling()))
-
-    def pass_on(step):
-        came_dred[step].wait_recv()
-        slot = ref["dredAll"].at[2 * step + place.k]
-        came_tokens.append(send(slot, slot, place.sibling()))
-
-    upstream = None
-    for member in range(4):
-        d_in = mm(ref["wm"][member * CH : (member + 1) * CH, :], d_reduced, NT).astype(BF16)
-        term = mm(d_in, groups[member * 64 : (member + 1) * 64, :])
-        upstream = term if upstream is None else upstream + term
+    came_half = [[], []]
+    for part in range(2):
+        ref["dredAll"][part, place.k] = d_reduced[:, part * CH : (part + 1) * CH]
+        own = ref["dredAll"].at[part, place.k]
+        for step in (2, 1, 3):
+            slot = ref["dredAll"].at[part, 2 * step + place.k]
+            came_dred[part, step] = send(own, slot, place.along("x", step))
+        came_half[part].append(send(own, own, place.sibling()))
+
+    def pass_on(part):
+        for step in (1, 3, 2):
+            came_dred[part, step].wait_recv()
+            slot = ref["dredAll"].at[part, 2 * step + place.k]
+            came_half[part].append(send(slot, slot, place.sibling()))
+
+    def merge_grads(part):
+        if part == 0:
+            for copy in came_tokens:
+                copy.wait_recv()
+        for copy in came_half[part]:
+            copy.wait_recv()
+        tokens = ref["gathAll"][...].reshape(8 * MTOK, 256)
+        grads = mm(tokens, ref["dredAll"][part].reshape(8 * MTOK, CH), TN).reshape(8, 4, 8, CH)
+        shares = jnp.concatenate([grads[..., :256], grads[..., 256:]], axis=2).astype(BF16)
+        for y in range(4):
+            ref["ms1"][part, y] = shares[:, y]
+        return start_stage(ref["ms1"].at[part], ref["mr1"].at[part], "y")
+
+    d_in = [
+        mm(d_reduced, ref["wm"][member * CH : (member + 1) * CH, :], NT).astype(BF16)
+        for member in range(4)
+    ]
+    upstream = mm(jnp.concatenate(d_in, axis=0), groups, TN)
     ref["upT"][...] = upstream
     a_scaled = upstream * gain
     a_mean = jnp.mean(a_scaled, axis=0, keepdims=True)
@@ -411,6 +425,13 @@
                 ref["qs3"][half, 4 * zh : 4 * zh + 4] = total.astype(BF16)
 
     q_stage = []
+    m_copies = []
+
+    def second_m(part):
+        ref["ms2"][part] = end_stage(
+            ref["ms1"].at[part], ref["mr1"].at[part], "y", m_copies[part]
+        ).astype(BF16)
+        m_copies[part] = start_stage(ref["ms2"].at[part], ref["mr2"].at[part], "z")
 
     d_attended = mm(ref["wp"][...], ref["dproj"][...]).astype(BF16)
     ref["dA"][...] = d_attended
@@ -449,15 +470,12 @@
     came_mix = []
     for half in range(2):
 
-        @pl.loop(half * 2, half * 2 + 2)
-        def _(group):
-            for inner in range(4):
-                attend_back(group * 4 + inner)
+        for h in range(8):
+            attend_back(half * 8 + h)
 
         came_mix.append(send(ref["dmix"].at[half], ref["dmixGot"].at[half], place.sibling()))
         if half == 0:
-            pass_on(1)
-            pass_on(3)
+            pass_on(0)
             came_rows.wait_recv()
             came_att.wait_recv()
             came_dproj.wait_recv()
@@ -469,7 +487,8 @@
                 put(0, 12 + 2 * piece, part[:128])
                 put(1, 12 + 2 * piece, part[128:])
         else:
-            pass_on(2)
+            m_copies.append(merge_grads(0))
+            pass_on(1)
             d_rows = None
             for block in range(6):
                 cols = slice((block % 3) * 512 + (block // 3) * 256, (block % 3) * 512 + (block // 3) * 256 + 256)
@@ -494,19 +513,13 @@
                 ref["qs1"][half, 0, first, second] = share[:4]
                 ref["qs1"][half, 1, second, first] = share[4:]
         q_stage.append(start_q(half, 0))
-    for copy in came_tokens:
-        copy.wait_recv()
-    tokens = ref["gathAll"][...].reshape(8 * MTOK, 256)
-    grads = mm(tokens, ref["dredAll"][...].reshape(8 * MTOK, WIDE), TN).reshape(8, 4, 8, WIDE)
-    shares = jnp.concatenate([grads[..., :512], grads[..., 512:]], axis=2).astype(BF16)
-    for y in range(4):
-        ref["ms1"][y] = shares[:, y]
-    m_copies = start_stage(ref["ms1"], ref["mr1"], "y")
+    m_copies.append(merge_grads(1))
 
     end_q(0, 0)
     q_stage[0] = start_q(0, 1)
     end_q(1, 0)
     q_stage[1] = start_q(1, 1)
+    second_m(0)
 
     for copy in came_o:
         copy.wait_recv()
@@ -516,8 +529,7 @@
     q_stage[0] = start_q(0, 2)
     end_q(1, 1)
     q_stage[1] = start_q(1, 2)
-    ref["ms2"][...] = end_stage(ref["ms1"], ref["mr1"], "y", m_copies).astype(BF16)
-    m_copies = start_stage(ref["ms2"], ref["mr2"], "z")
+    second_m(1)
 
     for copy in came_i:
         copy.wait_recv()
@@ -530,11 +542,12 @@
                 row, unit = parity * 12 + part * 4 + half * 2, parity * 6 + part * 2
                 ref["gqkv"][row : row + 2, :] = total[unit : unit + 2]
         ref["gproj"][half * 4 : half * 4 + 4, :] = total[12:]
-    total = end_stage(ref["ms2"], ref["mr2"], "z", m_copies) * factor
-    for fold in range(2):
-        for lane in range(4):
-            part = total[fold * 8 : fold * 8 + 8, lane * 128 : (lane + 1) * 128]
-            ref["gmerge"][pl.ds(fold * 4 + lane, 8, stride=8), :] = part
+    for half in range(2):
+        total = end_stage(ref["ms2"].at[half], ref["mr2"].at[half], "z", m_copies[half]) * factor
+        for fold in range(2):
+            for lane in range(2):
+                part = total[fold * 8 : fold * 8 + 8, lane * 128 : (lane + 1) * 128]
+                ref["gmerge"][pl.ds(half * 4 + fold * 2 + lane, 8, stride=8), :] = part
     for copy in pending:
         copy.wait_send()
     assert used[0] <= COPIES

time: 66.1 us -> 60.3 us (0.912)
  Pallas kernels: 65.3 us -> 59.4 us
    pallas_call x1, Pallas kernels: 63.5 us -> 57.6 us  [per_device(): pl.pallas_call(functools.partial(kernel, factor), name='block', out_shape...]
where the time goes in v2:
time: 60.3 us; the launch traced here: 60 us
  Pallas kernels  59.4 us (99%)
  between operations  0.65 us (1%)
    pallas_call x1, Pallas kernels, per_device(): pl.pallas_call(functools.partial(kernel, factor), name='block', out_shape...  57.6 us
    pallas_call x1, Pallas kernels, hand_over(): pl.pallas_call(copy_out, name='results', out_shape=tuple((jax.ShapeDtypeS...  1.76 us

profile of v2, /device:TPU:1, one launch (start us, length us, event | category | flops | bytes accessed | tf_op | source)
XLA Modules:
  0.0 60.0 jit_solution(1845136209591044661)
XLA Ops:
  0.6 57.6 %block.1 = (bf16[64,1024]{1,0:T(8,128)(2,1)}, bf16[256,512]{1,0:T(8,128)(2,1)}, f32[24,128]{1,0:T(8,128)}, f32[8,128]{1,0:T(8,128)}, f32[64,128]{1,0:T(8,128)}) custom-call(bf16[256,512]{1,0:T(8,128)(2,1)} %bitcast.12, bf16[64,1024]{1,0:T(8,128)(2,1)} %bitcast.13, bf16[512,1536]{1,0:T(8,128)(2,1)} %refs_2_.1, bf16[512,512]{1,0:T(8,128)(2,1)} %refs_3_.1, ...), custom_call_target="tpu_custom_call" | custom-call | tf_op jit(solution)/shard_map/block/pallas_call | solution.py:629
  58.3 1.8 %results.1 = (bf16[64,1024]{1,0:T(8,128)(2,1)}, bf16[256,512]{1,0:T(8,128)(2,1)}, f32[24,128]{1,0:T(8,128)}, f32[8,128]{1,0:T(8,128)}, f32[64,128]{1,0:T(8,128)}) custom-call(bf16[64,1024]{1,0:T(8,128)(2,1)} %get-tuple-element.15.refs_0_, bf16[256,512]{1,0:T(8,128)(2,1)} %get-tuple-element.16.refs_1_, f32[24,128]{1,0:T(8,128)} %get-tuple-element.17.refs_2_, ...), custom_call_target="tpu_custom_call" | custom-call | tf_op jit(solution)/shard_map/results/pallas_call | solution.py:601

commit v3 on v2

--- a/solution.py
+++ b/solution.py
@@ -146,10 +146,14 @@
     "gath": ((4, 2, MTOK, 256), BF16),
     "gathAll": ((8, MTOK, 256), BF16),
     "dredAll": ((2, 8, MTOK, CH), BF16),
-    "ms1": ((2, 4, 8, 16, 256), BF16),
-    "mr1": ((2, 3, 8, 16, 256), BF16),
-    "ms2": ((2, 8, 16, 256), BF16),
-    "mr2": ((2, 7, 16, 256), BF16),
+    "ms1a": ((8, 4, 16, 256), BF16),
+    "mr1a": ((7, 4, 16, 256), BF16),
+    "ms2a": ((4, 16, 256), BF16),
+    "mr2a": ((3, 16, 256), BF16),
+    "ms1b": ((4, 8, 16, 256), BF16),
+    "mr1b": ((3, 8, 16, 256), BF16),
+    "ms2b": ((8, 16, 256), BF16),
+    "mr2b": ((7, 16, 256), BF16),
     "qs1": ((2, 2, 4, 4, 4, 16, 128), BF16),
     "qr1": ((2, 2, 3, 4, 4, 16, 128), BF16),
     "qs2": ((2, 2, 4, 4, 16, 128), BF16),
@@ -372,9 +376,12 @@
         tokens = ref["gathAll"][...].reshape(8 * MTOK, 256)
         grads = mm(tokens, ref["dredAll"][part].reshape(8 * MTOK, CH), TN).reshape(8, 4, 8, CH)
         shares = jnp.concatenate([grads[..., :256], grads[..., 256:]], axis=2).astype(BF16)
-        for y in range(4):
-            ref["ms1"][part, y] = shares[:, y]
-        return start_stage(ref["ms1"].at[part], ref["mr1"].at[part], "y")
+        if part == 0:
+            ref["ms1a"][...] = shares
+        else:
+            for y in range(4):
+                ref["ms1b"][y] = shares[:, y]
+        return start_stage(*m_refs(part, 0))
 
     d_in = [
         mm(d_reduced, ref["wm"][member * CH : (member + 1) * CH, :], NT).astype(BF16)
@@ -427,11 +434,14 @@
     q_stage = []
     m_copies = []
 
+    def m_refs(part, stage):
+        name = str(stage + 1) + "ab"[part]
+        return ref["ms" + name], ref["mr" + name], "zy"[part ^ stage]
+
     def second_m(part):
-        ref["ms2"][part] = end_stage(
-            ref["ms1"].at[part], ref["mr1"].at[part], "y", m_copies[part]
-        ).astype(BF16)
-        m_copies[part] = start_stage(ref["ms2"].at[part], ref["mr2"].at[part], "z")
+        total = end_stage(*m_refs(part, 0), m_copies[part])
+        ref["ms2" + "ab"[part]][...] = total.astype(BF16)
+        m_copies[part] = start_stage(*m_refs(part, 1))
 
     d_attended = mm(ref["wp"][...], ref["dproj"][...]).astype(BF16)
     ref["dA"][...] = d_attended
@@ -468,36 +478,11 @@
             folds[half][pl.ds(unit + lane, 128, stride=16), :] = part
 
     came_mix = []
-    for half in range(2):
-
-        for h in range(8):
-            attend_back(half * 8 + h)
-
+
+    def send_mix(half):
         came_mix.append(send(ref["dmix"].at[half], ref["dmixGot"].at[half], place.sibling()))
-        if half == 0:
-            pass_on(0)
-            came_rows.wait_recv()
-            came_att.wait_recv()
-            came_dproj.wait_recv()
-            own_att = ref["attP"][place.k]
-            for piece in range(2):
-                cols = slice(piece * 256, (piece + 1) * 256)
-                part = mm(own_att, ref["dproj"][cols, :], NT)
-                part = part + mm(ref["attGot"][...], ref["dprojGot"][cols, :], NT)
-                put(0, 12 + 2 * piece, part[:128])
-                put(1, 12 + 2 * piece, part[128:])
-        else:
-            m_copies.append(merge_grads(0))
-            pass_on(1)
-            d_rows = None
-            for block in range(6):
-                cols = slice((block % 3) * 512 + (block // 3) * 256, (block % 3) * 512 + (block // 3) * 256 + 256)
-                rows = slice((block % 3) * 256, (block % 3) * 256 + 256)
-                term = mm(ref["wq"][:, cols], ref["dmix"][block // 3, rows, :])
-                d_rows = term if d_rows is None else d_rows + term
-            d_image = (ref["upT"][...] + d_rows).astype(BF16)
-            ref["sentI"][...] = mm(to_quads, d_image, NT).astype(BF16).reshape(4, 64, CH)
-            came_i = to_image("sentI", "gotI")
+
+    def q_grads(half):
         came_mix[half].wait_recv()
         own_rows = ref["rows"][place.k]
         for part in range(3):
@@ -513,23 +498,57 @@
                 ref["qs1"][half, 0, first, second] = share[:4]
                 ref["qs1"][half, 1, second, first] = share[4:]
         q_stage.append(start_q(half, 0))
-    m_copies.append(merge_grads(1))
-
+
+    for h in range(8):
+        attend_back(h)
+    send_mix(0)
+    came_rows.wait_recv()
+    came_att.wait_recv()
+    came_dproj.wait_recv()
+    own_att = ref["attP"][place.k]
+    for piece in range(2):
+        cols = slice(piece * 256, (piece + 1) * 256)
+        part = mm(own_att, ref["dproj"][cols, :], NT)
+        part = part + mm(ref["attGot"][...], ref["dprojGot"][cols, :], NT)
+        put(0, 12 + 2 * piece, part[:128])
+        put(1, 12 + 2 * piece, part[128:])
+    for h in range(8, 12):
+        attend_back(h)
+    q_grads(0)
+    pass_on(0)
+    for h in range(12, 16):
+        attend_back(h)
+    send_mix(1)
+    m_copies.append(merge_grads(0))
+    q_grads(1)
+    pass_on(1)
     end_q(0, 0)
     q_stage[0] = start_q(0, 1)
+
+    d_rows = None
+    for block in range(6):
+        cols = slice((block % 3) * 512 + (block // 3) * 256, (block % 3) * 512 + (block // 3) * 256 + 256)
+        rows = slice((block % 3) * 256, (block % 3) * 256 + 256)
+        term = mm(ref["wq"][:, cols], ref["dmix"][block // 3, rows, :])
+        d_rows = term if d_rows is None else d_rows + term
+    d_image = (ref["upT"][...] + d_rows).astype(BF16)
+    ref["sentI"][...] = mm(to_quads, d_image, NT).astype(BF16).reshape(4, 64, CH)
+    came_i = to_image("sentI", "gotI")
+    m_copies.append(merge_grads(1))
+
+    end_q(0, 1)
+    q_stage[0] = start_q(0, 2)
     end_q(1, 0)
     q_stage[1] = start_q(1, 1)
+    second_m(1)
     second_m(0)
 
     for copy in came_o:
         copy.wait_recv()
     ref["merged"][...] = mm(merged_back, ref["gotO"][...].reshape(MTOK, WIDE)).astype(BF16)
 
-    end_q(0, 1)
-    q_stage[0] = start_q(0, 2)
     end_q(1, 1)
     q_stage[1] = start_q(1, 2)
-    second_m(1)
 
     for copy in came_i:
         copy.wait_recv()
@@ -543,7 +562,7 @@
                 ref["gqkv"][row : row + 2, :] = total[unit : unit + 2]
         ref["gproj"][half * 4 : half * 4 + 4, :] = total[12:]
     for half in range(2):
-        total = end_stage(ref["ms2"].at[half], ref["mr2"].at[half], "z", m_copies[half]) * factor
+        total = end_stage(*m_refs(half, 1), m_copies[half]) * factor
         for fold in range(2):
             for lane in range(2):
                 part = total[fold * 8 : fold * 8 + 8, lane * 128 : (lane + 1) * 128]

time: 60.3 us -> 56.5 us (0.937)
  Pallas kernels: 59.4 us -> 55.7 us
    pallas_call x1, Pallas kernels: 57.6 us -> 53.9 us  [per_device(): pl.pallas_call(functools.partial(kernel, factor), name='block', out_shape...]
where the time goes in v3:
time: 56.5 us; the launch traced here: 56.4 us
  Pallas kernels  55.7 us (99%)
  between operations  0.65 us (1%)
    pallas_call x1, Pallas kernels, per_device(): pl.pallas_call(functools.partial(kernel, factor), name='block', out_shape...  53.9 us
    pallas_call x1, Pallas kernels, hand_over(): pl.pallas_call(copy_out, name='results', out_shape=tuple((jax.ShapeDtypeS...  1.76 us

profile of v3, /device:TPU:1, one launch (start us, length us, event | category | flops | bytes accessed | tf_op | source)
XLA Modules:
  0.0 56.4 jit_solution(16109623740978613309)
XLA Ops:
  0.6 53.9 %block.1 = (bf16[64,1024]{1,0:T(8,128)(2,1)}, bf16[256,512]{1,0:T(8,128)(2,1)}, f32[24,128]{1,0:T(8,128)}, f32[8,128]{1,0:T(8,128)}, f32[64,128]{1,0:T(8,128)}) custom-call(bf16[256,512]{1,0:T(8,128)(2,1)} %bitcast.12, bf16[64,1024]{1,0:T(8,128)(2,1)} %bitcast.13, bf16[512,1536]{1,0:T(8,128)(2,1)} %refs_2_.1, bf16[512,512]{1,0:T(8,128)(2,1)} %refs_3_.1, ...), custom_call_target="tpu_custom_call" | custom-call | tf_op jit(solution)/shard_map/block/pallas_call | solution.py:648
  54.6 1.8 %results.1 = (bf16[64,1024]{1,0:T(8,128)(2,1)}, bf16[256,512]{1,0:T(8,128)(2,1)}, f32[24,128]{1,0:T(8,128)}, f32[8,128]{1,0:T(8,128)}, f32[64,128]{1,0:T(8,128)}) custom-call(bf16[64,1024]{1,0:T(8,128)(2,1)} %get-tuple-element.15.refs_0_, bf16[256,512]{1,0:T(8,128)(2,1)} %get-tuple-element.16.refs_1_, f32[24,128]{1,0:T(8,128)} %get-tuple-element.17.refs_2_, ...), custom_call_target="tpu_custom_call" | custom-call | tf_op jit(solution)/shard_map/results/pallas_call | solution.py:620

commit v4 on v3

--- a/solution.py
+++ b/solution.py
@@ -193,14 +193,14 @@
     for axis, size in AXES.items():
         greeted += [place.along(axis, step) for step in range(1, size)]
     greeted += [place.along("x", step, 1 - place.k) for step in range(1, 4)]
-    barrier = pltpu.get_barrier_semaphore()
-    for device in greeted:
-        pl.semaphore_signal(barrier, inc=1, device_id=device, device_id_type=MESH)
-
     loads = {}
     for index, (src, dst) in enumerate(LOADS):
         loads[dst] = pltpu.make_async_copy(ref[src], ref[dst], ref["lsem"].at[index])
         loads[dst].start()
+
+    barrier = pltpu.get_barrier_semaphore()
+    for device in greeted:
+        pl.semaphore_signal(barrier, inc=1, device_id=device, device_id_type=MESH)
 
     t, n = iotas((TOK, TOK))
     to_quads = onehot(n == quad_source(t))
@@ -483,12 +483,12 @@
         came_mix.append(send(ref["dmix"].at[half], ref["dmixGot"].at[half], place.sibling()))
 
     def q_grads(half):
+        own_rows = ref["rows"][place.k]
+        spans = [slice(part * 256, (part + 1) * 256) for part in range(3)]
+        own = [mm(own_rows, ref["dmix"][half, cols, :], NT) for cols in spans]
         came_mix[half].wait_recv()
-        own_rows = ref["rows"][place.k]
-        for part in range(3):
-            cols = slice(part * 256, (part + 1) * 256)
-            values = mm(own_rows, ref["dmix"][half, cols, :], NT)
-            values = values + mm(ref["rowsGot"][...], ref["dmixGot"][half, cols, :], NT)
+        for part, cols in enumerate(spans):
+            values = own[part] + mm(ref["rowsGot"][...], ref["dmixGot"][half, cols, :], NT)
             put(half, 2 * part, values[:128])
             put(half, 6 + 2 * part, values[128:])
         for first in range(4):

time: 56.5 us -> 56.4 us (level)
  no operation moved by 1% of the time
where the time goes in v4:
time: 56.4 us; the launch traced here: 56.2 us
  Pallas kernels  55.6 us (99%)
  between operations  0.65 us (1%)
    pallas_call x1, Pallas kernels, per_device(): pl.pallas_call(functools.partial(kernel, factor), name='block', out_shape...  53.8 us
    pallas_call x1, Pallas kernels, hand_over(): pl.pallas_call(copy_out, name='results', out_shape=tuple((jax.ShapeDtypeS...  1.76 us

profile of v4, /device:TPU:1, one launch (start us, length us, event | category | flops | bytes accessed | tf_op | source)
XLA Modules:
  0.0 56.2 jit_solution(1053140403876305792)
XLA Ops:
  0.6 53.8 %block.1 = (bf16[64,1024]{1,0:T(8,128)(2,1)}, bf16[256,512]{1,0:T(8,128)(2,1)}, f32[24,128]{1,0:T(8,128)}, f32[8,128]{1,0:T(8,128)}, f32[64,128]{1,0:T(8,128)}) custom-call(bf16[256,512]{1,0:T(8,128)(2,1)} %bitcast.12, bf16[64,1024]{1,0:T(8,128)(2,1)} %bitcast.13, bf16[512,1536]{1,0:T(8,128)(2,1)} %refs_2_.1, bf16[512,512]{1,0:T(8,128)(2,1)} %refs_3_.1, ...), custom_call_target="tpu_custom_call" | custom-call | tf_op jit(solution)/shard_map/block/pallas_call | solution.py:648
  54.5 1.8 %results.1 = (bf16[64,1024]{1,0:T(8,128)(2,1)}, bf16[256,512]{1,0:T(8,128)(2,1)}, f32[24,128]{1,0:T(8,128)}, f32[8,128]{1,0:T(8,128)}, f32[64,128]{1,0:T(8,128)}) custom-call(bf16[64,1024]{1,0:T(8,128)(2,1)} %get-tuple-element.15.refs_0_, bf16[256,512]{1,0:T(8,128)(2,1)} %get-tuple-element.16.refs_1_, f32[24,128]{1,0:T(8,128)} %get-tuple-element.17.refs_2_, ...), custom_call_target="tpu_custom_call" | custom-call | tf_op jit(solution)/shard_map/results/pallas_call | solution.py:620
